TPU v7x, 512 devices: a whole 4x8x8 slice. The times are simulated.
512 devices in a mesh: dom: 64 (over z, y), rep: 8 (over x, core).
Axes of the slice: x: 4, y: 8, z: 8, core: 2. Of those that a mesh axis runs over, the one named last changes fastest.
Arguments:
- agg_feats: bfloat16 [65536, 256], P(('dom', 'rep')), may hold values from -6 to 6
- out_grad: bfloat16 [65536, 256], P(('dom', 'rep')), may hold values from -3 to 3
- w_in: bfloat16 [256, 256], replicated, may hold values from -0.375 to 0.375
- w_out: bfloat16 [256, 256], replicated, may hold values from -0.375 to 0.375
- bias_in: float32 [256], replicated, may hold values from -3 to 3
- self_weight: float32 [1], replicated, may hold values from 0 to 0.5
- mirror_rows: int32 [64, 8, 64, 32], P('dom', 'rep'), may hold values from 0 to 1023, as said below
- edge_src: int32 [64, 8, 4096], P('dom', 'rep'), may hold values from 0 to 3071, as said below
- edge_dst: int32 [64, 8, 4096], P('dom', 'rep'), may hold values from 0 to 3071
Outputs:
- grad_nodes: float32 [65536, 256], P(('dom', 'rep'))
- grad_w_in: float32 [256, 256], replicated
- grad_w_out: float32 [256, 256], replicated
- grad_bias: float32 [256], replicated
Inputs may be any that keep to these rules, and one draw needn't show every extreme that they name: `mirror_rows`: for device (d, r) and group k the 32 rows are distinct and lie among the masters of device (k, r), rows r * 128 to (r + 1) * 128 - 1. `edge_src`: on each device exactly 256 edges have a source among the masters of each device of its group (rows q * 128 to (q + 1) * 128 - 1 for q below 8); the other half of the edges have a mirror slot as source.
All inputs are finite; a program needn't handle non-finite values.
Results may differ from a plain program's by a relative error of at most 0.008.
Values may be sent and summed in bfloat16 or wider, within the bound.
A program may use at most 64 MiB of HBM per device.

v0:
```python
import jax
import jax.numpy as jnp
from jax import lax
from jax.sharding import PartitionSpec as P


def body(agg_feats, out_grad, w_in, w_out, bias_in, self_weight, mirror_rows, edge_src, edge_dst):
    preact = jnp.dot(agg_feats, w_in, preferred_element_type=jnp.float32) + bias_in
    gated = jax.nn.sigmoid(preact)
    activated = (preact * gated).astype(jnp.bfloat16)
    back_act = lax.dot_general(
        out_grad, w_out, (((1,), (1,)), ((), ())), preferred_element_type=jnp.float32
    )
    grad_pre = (back_act * gated * (1.0 + preact * (1.0 - gated))).astype(jnp.bfloat16)
    grad_agg = lax.dot_general(
        grad_pre, w_in, (((1,), (1,)), ((), ())), preferred_element_type=jnp.float32
    ).astype(jnp.bfloat16)
    group = lax.all_gather(grad_agg, "rep", axis=0, tiled=True)
    group_size = group.shape[0]
    domains = lax.axis_size("dom")
    slot_count = mirror_rows.shape[3]
    width = group.shape[1]
    asked_rows = lax.all_to_all(mirror_rows[0, 0], "dom", split_axis=0, concat_axis=0, tiled=True)
    picked = jnp.take(group, asked_rows, axis=0)
    replied = lax.all_to_all(picked, "dom", split_axis=0, concat_axis=0, tiled=True)
    mirror_vals, asked_rows = (replied, asked_rows)
    norm_scale = float(group_size * domains) ** (-0.5)
    grad_w_out = (
        lax.dot_general(
            activated, out_grad, (((0,), (0,)), ((), ())), preferred_element_type=jnp.float32
        )
        * norm_scale
    )
    grad_w_in = (
        lax.dot_general(
            agg_feats, grad_pre, (((0,), (0,)), ((), ())), preferred_element_type=jnp.float32
        )
        * norm_scale
    )
    grad_bias = jnp.sum(grad_pre.astype(jnp.float32), axis=0) * norm_scale
    grad_w_in, grad_w_out, grad_bias = lax.psum((grad_w_in, grad_w_out, grad_bias), ("dom", "rep"))
    table = jnp.concatenate([group, mirror_vals.reshape(domains * slot_count, width)], axis=0)
    sources = edge_src.reshape(-1)
    targets = edge_dst.reshape(-1)
    fetched = jnp.take(table, targets, axis=0)
    mirror_total = domains * slot_count
    gathered = fetched.astype(jnp.float32)
    totals = jax.ops.segment_sum(gathered, sources, group_size + mirror_total)
    returned = lax.all_to_all(
        totals[group_size:].reshape(domains, slot_count, width),
        "dom",
        split_axis=0,
        concat_axis=0,
        tiled=True,
    )
    group_part = totals[:group_size]
    group_part = group_part + jax.ops.segment_sum(
        returned.reshape(-1, width), asked_rows.reshape(-1), group_size
    )
    owned = lax.psum_scatter(group_part, "rep", scatter_dimension=0, tiled=True)
    grad_nodes = (1.0 + self_weight[0]) * grad_agg.astype(jnp.float32) + owned
    return (grad_nodes, grad_w_in, grad_w_out, grad_bias)


def solution(mesh):
    placed = (
        P(("dom", "rep"), None),
        P(("dom", "rep"), None),
        P(),
        P(),
        P(),
        P(),
        P("dom", "rep", None, None),
        P("dom", "rep", None),
        P("dom", "rep", None),
    )
    return jax.shard_map(
        body,
        mesh=mesh,
        in_specs=placed,
        out_specs=(P(("dom", "rep"), None), P(), P(), P()),
        check_vma=False,
    )
```

profile of v0, /device:TPU:17, one launch (start us, length us, event | category | flops | bytes accessed | tf_op | source)
XLA Modules:
  0.0 471.9 jit_solution(10917993535643128448)
XLA Ops:
  8.0 0.0 copy-start
  8.0 1.4 copy.19
  9.5 15.9 %all-to-all-start = ((s32[64,1,32]{2,1,0:T(1,128)}), s32[64,1,32]{2,1,0:T(1,128)S(1)}, u32[]{:S(2)}, u32[]{:S(2)}) async-start(s32[64,1,32]{2,1,0:T(1,128)} %bitcast.3), calls=%async_computation | async-start | bytes 65536 | tf_op jit(solution)/shard_map/all_to_all | solution.py:23
  25.4 0.0 copy-done
  25.4 1.0 convolution_add_fusion
  26.4 0.0 copy-start.4
  26.4 1.2 convert_reduce_fusion
  27.6 0.2 convolution_convert_fusion
  27.8 0.0 copy-done.4
  27.8 14.5 %all_gather.3 = bf16[1024,256]{1,0:T(8,128)(2,1)S(1)} all-gather(bf16[128,256]{1,0:T(8,128)(2,1)S(1)} %convolution_convert_fusion), channel_id=1, replica_groups=mesh['dom'=64,'rep'=8] {'rep'}, dimensions={0}, use_global_device_ids=true | all-gather | bytes 589824 | tf_op jit(solution)/shard_map/all_gather | solution.py:18
  42.4 0.0 all-to-all-done
  42.4 0.1 reshape.104
  42.5 7.5 %gather_fusion = bf16[2048,256]{1,0:T(8,128)(2,1)S(1)} fusion(bf16[1024,256]{1,0:T(8,128)(2,1)S(1)} %all_gather.3, s32[2048]{0:T(1024)S(1)} %broadcast_clamp_fusion.1), kind=kCustom, calls=%fused_computation | custom fusion | bytes 2105344 | tf_op jit(solution)/shard_map/jit(_take)/gather | solution.py:24
  50.0 0.0 copy-start.5
  50.0 1.2 broadcast_select_fusion
  51.2 12.1 %all-to-all-start.1 = ((bf16[64,32,256]{2,1,0:T(8,128)(2,1)}), bf16[64,32,256]{2,1,0:T(8,128)(2,1)S(1)}, u32[]{:S(2)}, u32[]{:S(2)}) async-start(bf16[64,32,256]{2,1,0:T(8,128)(2,1)} %broadcast_select_fusion), calls=%async_computation.1 | async-start | bytes 2097152 | tf_op jit(solution)/shard_map/all_to_all | solution.py:25
  63.4 0.0 copy-done.5
  63.5 28.0 %all-to-all-done.1 = bf16[64,32,256]{2,1,0:T(8,128)(2,1)S(1)} async-done(((bf16[64,32,256]{2,1,0:T(8,128)(2,1)}), bf16[64,32,256]{2,1,0:T(8,128)(2,1)S(1)}, u32[]{:S(2)}, u32[]{:S(2)}) %all-to-all-start.1) | async-done | bytes 1048608 | tf_op jit(solution)/shard_map/all_to_all | solution.py:25
  91.5 1.3 pad_maximum_fusion
  92.8 53.8 %scatter_custom_fusion = f32[3072,256]{1,0:T(8,128)S(1)} fusion(s32[4096]{0:T(1024)} %bitcast.34, pred[4096]{0:T(1024)(128)(4,1)S(1)} %compare_and_fusion.1, f32[]{:T(128)} %constant.21.clone.1, bf16[]{:T(256)} %constant.40.clone.1, bf16[3072,256]{1,0:T(8,128)(2,1)} %pad_maximum_fusion, s32[4096]{0:T(1024)S(1)} %broadcast_clamp_fusion), kind=kCustom, calls=%fused_computation.4 | custom fusion | flops 3145728 | bytes 4740096 | tf_op jit(solution)/shard_map/scatter-add | solution.py:48
  146.6 0.0 copy-start.2
  146.6 1.6 slice.13
  148.2 0.7 copy-done.2
  148.9 0.0 copy-start.3
  148.9 8.1 %all-to-all-start.2 = ((f32[64,32,256]{2,1,0:T(8,128)}), f32[64,32,256]{2,1,0:T(8,128)S(1)}, u32[]{:S(2)}, u32[]{:S(2)}) async-start(f32[64,32,256]{2,1,0:T(8,128)} %bitcast.27), calls=%async_computation.2 | async-start | bytes 4194304 | tf_op jit(solution)/shard_map/all_to_all | solution.py:49
  157.1 0.0 all-reduce.3.cloned.1.call-start
  157.1 0.0 copy-done.3
  157.1 0.9 fusion.5
  158.0 1.9 convolution_multiply_fusion
  159.9 0.0 all-reduce.3.cloned.1.call-update
  159.9 0.0 reduce-scatter.2.cloned.1.call-start
  160.0 0.5 broadcast.77
  160.5 0.7 reduce.3
  161.2 0.1 reshape.128
  161.3 1.3 slice.12
  162.6 43.5 %all-to-all-done.2 = f32[64,32,256]{2,1,0:T(8,128)S(1)} async-done(((f32[64,32,256]{2,1,0:T(8,128)}), f32[64,32,256]{2,1,0:T(8,128)S(1)}, u32[]{:S(2)}, u32[]{:S(2)}) %all-to-all-start.2) | async-done | bytes 2097184 | tf_op jit(solution)/shard_map/all_to_all | solution.py:49
  206.1 12.1 %scatter_fusion = f32[1024,256]{1,0:T(8,128)S(1)} fusion(f32[1024,256]{1,0:T(8,128)S(1)} %slice.12, s32[2048]{0:T(1024)S(1)} %reshape.128, f32[2048,256]{1,0:T(8,128)S(1)} %bitcast.26), kind=kCustom, calls=%fused_computation.3 | custom fusion | flops 524288 | bytes 6299648 | tf_op jit(solution)/shard_map/scatter-add | solution.py:57
  218.2 0.0 copy-start.1
  218.3 1.0 copy-done.1
  219.2 0.0 reduce-scatter.2.cloned.1.call-update
  219.9 100.7 %psum.23 = f32[256]{0:T(256)} all-reduce(f32[256]{0:T(256)S(1)} %broadcast_multiply_fusion), channel_id=1, replica_groups=mesh['dom'=64,'rep'=8] {'dom','rep'}, use_global_device_ids=true, to_apply=%region_6.7 | all-reduce | flops 256 | bytes 2048 | tf_op jit(solution)/shard_map/psum | solution.py:41
  320.6 138.9 %all-reduce.3.cloned.1.call-done = (f32[256,256]{0,1:T(8,128)}, f32[256,256]{1,0:T(8,128)}) async-done(((f32[256,256]{0,1:T(8,128)}, f32[256,256]{1,0:T(8,128)}), (f32[256,256]{0,1:T(8,128)}, f32[256,256]{1,0:T(8,128)})) %all-reduce.3.cloned.1.call-update) | async-done | bytes 524304 | tf_op jit(solution)/shard_map/psum | solution.py:41
  459.5 1.8 copy.20
  461.2 0.0 reduce-scatter.2.cloned.1.call-done
  461.3 1.6 multiply_add_fusion
  462.8 1.7 copy.25
  (7 shorter events, 0.1 us)
Async XLA Ops:
  8.0 17.4 %copy-start = (bf16[256,256]{1,0:T(8,128)(2,1)S(1)}, bf16[256,256]{1,0:T(8,128)(2,1)}, u32[]{:S(2)}) copy-start(bf16[256,256]{1,0:T(8,128)(2,1)} %param.11) | copy-start | bytes 393220
  9.5 32.9 %all-to-all-start = ((s32[64,1,32]{2,1,0:T(1,128)}), s32[64,1,32]{2,1,0:T(1,128)S(1)}, u32[]{:S(2)}, u32[]{:S(2)}) async-start(s32[64,1,32]{2,1,0:T(1,128)} %bitcast.3), calls=%async_computation | async-start | bytes 65536 | tf_op jit(solution)/shard_map/all_to_all | solution.py:23
  26.4 1.4 copy-start.4
  50.0 13.4 %copy-start.5 = (s32[1,1,4096]{2,1,0:T(1,128)S(1)}, s32[1,1,4096]{2,1,0:T(1,128)}, u32[]{:S(2)}) copy-start(s32[1,1,4096]{2,1,0:T(1,128)} %param.17) | copy-start | bytes 49156
  51.2 40.3 %all-to-all-start.1 = ((bf16[64,32,256]{2,1,0:T(8,128)(2,1)}), bf16[64,32,256]{2,1,0:T(8,128)(2,1)S(1)}, u32[]{:S(2)}, u32[]{:S(2)}) async-start(bf16[64,32,256]{2,1,0:T(8,128)(2,1)} %broadcast_select_fusion), calls=%async_computation.1 | async-start | bytes 2097152 | tf_op jit(solution)/shard_map/all_to_all | solution.py:25
  146.6 2.3 copy-start.2
  148.9 8.2 %copy-start.3 = (bf16[128,256]{1,0:T(8,128)(2,1)S(1)}, bf16[128,256]{1,0:T(8,128)(2,1)}, u32[]{:S(2)}) copy-start(bf16[128,256]{1,0:T(8,128)(2,1)} %param.9) | copy-start | bytes 196612
  148.9 57.2 %all-to-all-start.2 = ((f32[64,32,256]{2,1,0:T(8,128)}), f32[64,32,256]{2,1,0:T(8,128)S(1)}, u32[]{:S(2)}, u32[]{:S(2)}) async-start(f32[64,32,256]{2,1,0:T(8,128)} %bitcast.27), calls=%async_computation.2 | async-start | bytes 4194304 | tf_op jit(solution)/shard_map/all_to_all | solution.py:49
  157.1 302.4 %all-reduce.3.cloned.1.call-start = ((), (), s32[]{:S(2)}) async-start(), calls=%async_computation.5 | async-start | bytes 1048576 | tf_op jit(solution)/shard_map/psum | solution.py:41
  159.9 301.4 %reduce-scatter.2.cloned.1.call-start = ((), (), s32[]{:S(2)}) async-start(), calls=%async_computation.4 | async-start | bytes 1179648 | tf_op jit(solution)/shard_map/reduce_scatter | solution.py:60
  218.2 1.0 copy-start.1
Sparse Core Ops, SparseCore 0:
  163.6 295.7 all-reduce.2
Sparse Core Ops, SparseCore 1:
  219.3 35.4 reduce-scatter.1
where the time goes:
time: 473 us; the launch traced here: 472 us
  waiting for transfers between devices  211 us (45%)
  blocking collectives  115 us (24%)
  other arithmetic  70.8 us (15%)
  starting transfers between devices  36.3 us (8%)
  local copies, waits for them, and re-layouts  17.7 us (4%)
  between operations  16.3 us (3%)
  matrix products  5.17 us (1%)
    psum x1, waiting for transfers between devices, body(): lax.psum((grad_w_in, grad_w_out, grad_bias), ('dom', 'rep'))  139 us
    psum x1, blocking collectives, body(): lax.psum((grad_w_in, grad_w_out, grad_bias), ('dom', 'rep'))  101 us
    scatter-add x1, other arithmetic, body(): totals = jax.ops.segment_sum(gathered, sources, group_size + mirror_total)  53.8 us
    all_to_all x1, waiting for transfers between devices, body(): lax.all_to_all(totals[group_size:].reshape(domains, slot_count, width), '...  43.5 us
    all_to_all x1, waiting for transfers between devices, body(): lax.all_to_all(picked, 'dom', split_axis=0, concat_axis=0, tiled=True)  28 us
    all_to_all x1, starting transfers between devices, body(): lax.all_to_all(mirror_rows[0, 0], 'dom', split_axis=0, concat_axis=0, til...  15.9 us
    all_gather x1, blocking collectives, body(): group = lax.all_gather(grad_agg, 'rep', axis=0, tiled=True)  14.5 us
    all_to_all x1, starting transfers between devices, body(): lax.all_to_all(picked, 'dom', split_axis=0, concat_axis=0, tiled=True)  12.1 us
  transfers between devices with their start and end apart: 5, of which 3 were waited for; matrix products, arithmetic and copies ran while one was open for 5% of the time, Pallas kernels for 0%

commit v1 on v0

v1 whole, which is shorter than its diff:
```python
import functools

import jax
import jax.numpy as jnp
from jax import lax
from jax.experimental import pallas as pl
from jax.experimental.pallas import tpu as pltpu
from jax.sharding import PartitionSpec as P

MESH = pl.DeviceIdType.MESH
BF = jnp.bfloat16
F32 = jnp.float32

LINE = 8
ROWS = 128
SLOT = 32
HALF = 128
WIDE = 256
EDGES = 4096
ORDER = (0, 1, 7, 2, 6, 3, 5, 4)
FWD = ((0, 1), (7, 2), (6, 3), (5, 4))
BWD = ((0, 1), (7, 2), (6, 3), (5, 4))

STAGES = (
    "idx_a", "idx_b", "one_a", "one_b", "group", "w_rep", "b_rep", "w_z", "w_y", "w_zg", "w_repg",
    "back_a", "back_b", "gsum", "last_a", "last_b",
)
SEM = {name: i for i, name in enumerate(STAGES)}
TWO_A = len(STAGES)
TWO_B = TWO_A + len(FWD)
N_SEM = TWO_B + len(FWD)


def offset(i):
    odd = i % 2
    return (1 - odd) * ((i + 2) // 2) + odd * (LINE - (i + 1) // 2)


def times(count, step):
    def run(i, carry):
        step(i)
        return carry

    lax.fori_loop(0, count, run, 0)


def dot(a, b, dims=((1,), (0,))):
    return lax.dot_general(a, b, (dims, ((), ())), preferred_element_type=F32)


def kernel(
    agg_ref, og_ref, w_in_ref, w_out_ref, bias_ref, sw_ref, idx_a_ref, idx_b_ref, dst_ref, src_ref,
    nodes_ref, weights_ref, bsum_ref,
    ga_ref, grp, blk_a, blk_b, ia, ib, pt_a, pt_b, stage_a, stage_b, mir_a, mir_b,
    v_dst, v_src, wbuf, fetched, out_a, out_b, ra, rb, last_src_a, last_src_b, fa, fb, gout, gin,
    wsend, wrecv, bsend, brecv, zsend, zrecv, ysend, yrecv, zg, wfull, ssem, rsem,
):
    me = lax.axis_index("dom")
    r = lax.axis_index("rep")
    z, y = me // LINE, me % LINE

    def on_z(to):
        return (to * LINE + y, r)

    def on_y(to):
        return (z * LINE + to, r)

    def on_rep(to):
        return (me, to)

    def send(src, dst, sem, device):
        pltpu.make_async_remote_copy(
            src_ref=src, dst_ref=dst, send_sem=ssem.at[sem], recv_sem=rsem.at[sem],
            device_id=device, device_id_type=MESH,
        ).start()

    def got(view, sem):
        pltpu.make_async_copy(view, view, rsem.at[sem]).wait()

    def sent(view, sem):
        pltpu.make_async_copy(view, view, ssem.at[sem]).wait()

    barrier = pltpu.get_barrier_semaphore()

    def greet(i):
        for device in (on_z((z + i + 1) % LINE), on_y((y + i + 1) % LINE), on_rep((r + i + 1) % LINE)):
            pl.semaphore_signal(barrier, inc=1, device_id=device, device_id_type=MESH)

    times(LINE - 1, greet)

    agg, og = agg_ref[...], og_ref[...]
    preact = dot(agg, w_in_ref[...]) + bias_ref[...]
    gated = jax.nn.sigmoid(preact)
    back_act = dot(og, w_out_ref[...], ((1,), (1,)))
    grad_pre = (back_act * gated * (1.0 + preact * (1.0 - gated))).astype(BF)
    grad_agg = dot(grad_pre, w_in_ref[...], ((1,), (1,))).astype(BF)
    ga_ref[...] = grad_agg
    grp[r] = grad_agg
    blk_a[z] = grad_agg[:, :HALF]
    blk_b[y] = grad_agg[:, HALF:]
    ia[y] = idx_a_ref[y]
    ib[z] = idx_b_ref[z]

    pl.semaphore_wait(barrier, 3 * (LINE - 1))

    def send_idx(i):
        to = (y + offset(i)) % LINE
        send(idx_a_ref.at[to], ia.at[y], SEM["idx_a"], on_y(to))
        to = (z + offset(i)) % LINE
        send(idx_b_ref.at[to], ib.at[z], SEM["idx_b"], on_z(to))

    times(LINE - 1, send_idx)

    def send_blocks(i):
        send(blk_a.at[z], blk_a.at[z], SEM["one_a"], on_z((z + offset(i)) % LINE))
        send(blk_b.at[y], blk_b.at[y], SEM["one_b"], on_y((y + offset(i)) % LINE))
        send(grp.at[r], grp.at[r], SEM["group"], on_rep((r + i + 1) % LINE))

    times(LINE - 1, send_blocks)

    activated = (preact * gated).astype(BF)
    g_in = dot(agg, grad_pre, ((0,), (0,)))
    g_out = dot(activated, og, ((0,), (0,)))
    wsend[0:4] = g_in.reshape(4, 64, WIDE)
    wsend[4:8] = g_out.reshape(4, 64, WIDE)
    column_sums = jnp.sum(grad_pre.astype(F32), axis=0, keepdims=True)
    row = lax.broadcasted_iota(jnp.int32, (8, HALF), 0)
    bsend[...] = jnp.where(
        row == 0, column_sums[:, :HALF], jnp.where(row == 1, column_sums[:, HALF:], 0.0)
    )

    def send_weights(i):
        to = (r + i + 1) % LINE
        send(wsend.at[to], wrecv.at[r], SEM["w_rep"], on_rep(to))
        send(bsend, brecv.at[r], SEM["b_rep"], on_rep(to))

    times(LINE - 1, send_weights)
    wrecv[r] = wsend[r]
    brecv[r] = bsend[...]

    lane = lax.broadcasted_iota(jnp.int32, (ROWS, ROWS), 1)
    for c in range(EDGES // ROWS):
        col = dst_ref[:, c : c + 1]
        v_dst[c * ROWS : (c + 1) * ROWS, :] = jnp.where((col & 127) == lane, col >> 7, -1).astype(BF)
    sub = lax.broadcasted_iota(jnp.int32, (ROWS, 512), 0)
    for c in range(EDGES // 512):
        cut = src_ref[:, c * 512 : (c + 1) * 512]
        v_src[:, c * 512 : (c + 1) * 512] = jnp.where((cut & 127) == sub, cut >> 7, -1).astype(BF)

    def one_hot(codes, high):
        if not isinstance(high, int):
            high = high.astype(F32)
        return jnp.where(codes == jnp.asarray(high, F32).astype(BF), BF(1), BF(0))

    got(ia.at[0:7], SEM["idx_a"])
    got(ib.at[0:7], SEM["idx_b"])
    sub = lax.broadcasted_iota(jnp.int32, (ROWS, WIDE), 0)
    for asked, picks in ((ia, pt_a), (ib, pt_b)):
        parts = []
        for g in range(2):
            part = asked[4 * g]
            for i in range(1, 4):
                part = jnp.maximum(part, asked[4 * g + i])
            parts.append(part)
        both = jnp.concatenate(parts, axis=1)
        for i in range(LINE):
            picks[i] = jnp.where(sub == both[i : i + 1, :], 1.0, 0.0).astype(BF)

    got(blk_b.at[0:7], SEM["one_b"])

    def pick_b(i):
        rows = dot(pt_b[i], blk_b[i], ((0,), (0,))).astype(BF)
        stage_b[:, i] = rows.reshape(LINE, SLOT, HALF)

    times(LINE, pick_b)
    mir_b[z] = stage_b[z]
    got(blk_a.at[0:7], SEM["one_a"])

    def pick_a(i):
        rows = dot(pt_a[i], blk_a[i], ((0,), (0,))).astype(BF)
        stage_a[:, i] = rows.reshape(LINE, SLOT, HALF)

    times(LINE, pick_a)
    mir_a[:, y] = stage_a[y]
    for c, offsets in enumerate(FWD):
        for j in offsets:
            if j:
                to = (z + LINE - j) % LINE
                send(stage_b.at[to], mir_b.at[z], TWO_B + c, on_z(to))
            block = (z + j) % LINE

            def send_a(i, block=block, c=c):
                to = (y + offset(i)) % LINE
                send(stage_a.at[to, block], mir_a.at[block, y], TWO_A + c, on_y(to))

            times(LINE - 1, send_a)

    got(grp.at[0:7], SEM["group"])
    step = 512

    def gather_group(i):
        at = pl.ds(pl.multiple_of(i * step, step), step)
        codes = v_dst[at, :]
        hot = jnp.concatenate([one_hot(codes, h) for h in range(LINE)], axis=1)
        fetched[at, :] = dot(hot, grp[...].reshape(LINE * ROWS, WIDE)).astype(BF)

    times(EDGES // step, gather_group)

    got(wrecv.at[0:7], SEM["w_rep"])
    got(brecv.at[0:7], SEM["b_rep"])
    total = wrecv[0]
    bias_total = brecv[0]
    for i in range(1, LINE):
        total = total + wrecv[i]
        bias_total = bias_total + brecv[i]
    zsend[:, :, :WIDE] = total.reshape(LINE, 8, WIDE)
    zsend[:, :, WIDE:] = jnp.broadcast_to(bias_total[None], (LINE, 8, HALF))

    def send_z(i):
        to = (z + offset(i)) % LINE
        send(zsend.at[to], zrecv.at[z], SEM["w_z"], on_z(to))

    times(LINE - 1, send_z)
    zrecv[z] = zsend[z]

    def gather_mirrors(c):
        offsets = FWD[c]
        got(mir_b.at[0 : len([j for j in offsets if j])], TWO_B + c)
        got(mir_a.at[0 : len(offsets), 0:7], TWO_A + c)
        blocks = [(z + j) % LINE for j in offsets]
        for n, block in enumerate(blocks):
            wbuf[n * WIDE : (n + 1) * WIDE, :HALF] = mir_a[block].reshape(WIDE, HALF)
            wbuf[n * WIDE : (n + 1) * WIDE, HALF:] = mir_b[block].reshape(WIDE, HALF)
        depth = len(blocks) * WIDE
        highs = [8 + 2 * block + h for block in blocks for h in range(2)]

        def run(i):
            at = pl.ds(pl.multiple_of(i * step, step), step)
            codes = v_dst[at, :]
            hot = jnp.concatenate([one_hot(codes, h) for h in highs], axis=1)
            fetched[at, :] = fetched[at, :] + dot(hot, wbuf[:depth, :]).astype(BF)

        times(EDGES // step, run)

    gather_mirrors(0)

    got(zrecv.at[0:7], SEM["w_z"])
    total = zrecv[0]
    for i in range(1, LINE):
        total = total + zrecv[i]
    ysend[...] = total

    def send_y(i):
        send(ysend, yrecv.at[y], SEM["w_y"], on_y((y + offset(i)) % LINE))

    times(LINE - 1, send_y)
    yrecv[y] = total

    for c in range(1, len(FWD)):
        gather_mirrors(c)

    for offsets in BWD:
        blocks = [(z + j) % LINE for j in offsets]
        hot = jnp.concatenate(
            [one_hot(v_src[...], 8 + 2 * block + h) for block in blocks for h in range(2)], axis=0
        )
        sums = dot(hot, fetched[...]).astype(BF)
        for n, (j, block) in enumerate(zip(offsets, blocks)):
            part = sums[n * WIDE : (n + 1) * WIDE]
            out_a[block] = part[:, :HALF].reshape(LINE, SLOT, HALF)
            out_b[block] = part[:, HALF:].reshape(LINE, SLOT, HALF)
            if j:
                send(out_b.at[block], rb.at[z], SEM["back_b"], on_z(block))
            else:
                rb[z] = out_b[block]
            ra[y, block] = out_a[block, y]

            def send_back(i, block=block):
                to = (y + offset(i)) % LINE
                send(out_a.at[block, to], ra.at[y, block], SEM["back_a"], on_y(to))

            times(LINE - 1, send_back)

    got(yrecv.at[0:7], SEM["w_y"])
    total = yrecv[0]
    for i in range(1, LINE):
        total = total + yrecv[i]
    bsum_ref[...] = total[:, WIDE:]
    zg[z] = total[:, :WIDE]

    def send_zg(i):
        send(zg.at[z], zg.at[z], SEM["w_zg"], on_z((z + offset(i)) % LINE))

    times(LINE - 1, send_zg)

    for c in range(2):
        hot = jnp.concatenate([one_hot(v_src[...], 4 * c + h) for h in range(4)], axis=0)
        gout[4 * c : 4 * c + 4] = dot(hot, fetched[...]).astype(BF).reshape(4, ROWS, WIDE)

    def send_sums(i):
        to = (r + i + 1) % LINE
        send(gout.at[to], gin.at[r], SEM["gsum"], on_rep(to))

    times(LINE - 1, send_sums)
    gin[r] = gout[r]

    got(zg.at[0:7], SEM["w_zg"])
    wfull[r] = zg[...].reshape(64, WIDE)

    def send_full(i):
        send(wfull.at[r], wfull.at[r], SEM["w_repg"], on_rep((r + i + 1) % LINE))

    times(LINE - 1, send_full)

    got(rb.at[0:7], SEM["back_b"])

    def add_b(i):
        sums = dot(pt_b[i], rb[:, i].reshape(WIDE, HALF))
        last_src_b[i] = sums.astype(BF)

    times(LINE, add_b)
    fb[y] = last_src_b[y]

    def send_last_b(i):
        to = (y + offset(i)) % LINE
        send(last_src_b.at[to], fb.at[y], SEM["last_b"], on_y(to))

    times(LINE - 1, send_last_b)
    got(ra.at[0:7], SEM["back_a"])

    def add_a(i):
        sums = dot(pt_a[i], ra[:, i].reshape(WIDE, HALF))
        last_src_a[i] = sums.astype(BF)

    times(LINE, add_a)
    fa[z] = last_src_a[z]

    def send_last_a(i):
        to = (z + offset(i)) % LINE
        send(last_src_a.at[to], fa.at[z], SEM["last_a"], on_z(to))

    times(LINE - 1, send_last_a)

    nodes = (1.0 + sw_ref[0]) * ga_ref[...].astype(F32)
    got(gin.at[0:7], SEM["gsum"])
    for i in range(LINE):
        nodes = nodes + gin[i].astype(F32)
    got(wfull.at[0:7], SEM["w_repg"])
    weights_ref[...] = wfull[...].reshape(LINE * 64, WIDE)
    got(fb.at[0:7], SEM["last_b"])
    right = nodes[:, HALF:]
    for i in range(LINE):
        right = right + fb[i].astype(F32)
    nodes_ref[:, HALF:] = right
    got(fa.at[0:7], SEM["last_a"])
    left = nodes[:, :HALF]
    for i in range(LINE):
        left = left + fa[i].astype(F32)
    nodes_ref[:, :HALF] = left

    for view, name in (
        (ia, "idx_a"), (ib, "idx_b"), (blk_a, "one_a"), (blk_b, "one_b"), (grp, "group"), (wrecv, "w_rep"),
        (brecv, "b_rep"), (zrecv, "w_z"), (yrecv, "w_y"), (zg, "w_zg"), (wfull, "w_repg"), (ra, "back_a"),
        (rb, "back_b"), (gin, "gsum"), (fa, "last_a"), (fb, "last_b"),
    ):
        sent(view.at[0:7], SEM[name])
    for c, offsets in enumerate(FWD):
        sent(mir_b.at[0 : len([j for j in offsets if j])], TWO_B + c)
        sent(mir_a.at[0 : len(offsets), 0:7], TWO_A + c)


def body(agg_feats, out_grad, w_in, w_out, bias_in, self_weight, mirror_rows, edge_src, edge_dst):
    me = lax.axis_index("dom")
    r = lax.axis_index("rep")
    z, y = me // LINE, me % LINE
    rows = mirror_rows[0, 0] - r * ROWS
    rows = jnp.tile(rows, (1, 4)).reshape(LINE, LINE, ROWS)
    quarter = lax.broadcasted_iota(jnp.int32, (1, 1, ROWS), 2) // SLOT
    idx_a = jnp.where(quarter == y % 4, rows.swapaxes(0, 1), -1)
    idx_b = jnp.where(quarter == z % 4, rows, -1)
    dst = edge_dst.reshape(EDGES // ROWS, ROWS).T
    src = edge_src.reshape(1, EDGES)

    vmem = pl.BlockSpec(memory_space=pltpu.VMEM)
    smem = pl.BlockSpec(memory_space=pltpu.SMEM)
    V = pltpu.VMEM
    scratch = [
        V((ROWS, WIDE), BF),
        V((LINE, ROWS, WIDE), BF),
        V((LINE, ROWS, HALF), BF), V((LINE, ROWS, HALF), BF),
        V((LINE, LINE, ROWS), jnp.int32), V((LINE, LINE, ROWS), jnp.int32),
        V((LINE, ROWS, WIDE), BF), V((LINE, ROWS, WIDE), BF),
        V((LINE, LINE, SLOT, HALF), BF), V((LINE, LINE, SLOT, HALF), BF),
        V((LINE, LINE, SLOT, HALF), BF), V((LINE, LINE, SLOT, HALF), BF),
        V((EDGES, ROWS), BF), V((ROWS, EDGES), BF),
        V((max(map(len, FWD)) * WIDE, WIDE), BF),
        V((EDGES, WIDE), BF),
        V((LINE, LINE, SLOT, HALF), BF), V((LINE, LINE, SLOT, HALF), BF),
        V((LINE, LINE, SLOT, HALF), BF), V((LINE, LINE, SLOT, HALF), BF),
        V((LINE, ROWS, HALF), BF), V((LINE, ROWS, HALF), BF),
        V((LINE, ROWS, HALF), BF), V((LINE, ROWS, HALF), BF),
        V((LINE, ROWS, WIDE), BF), V((LINE, ROWS, WIDE), BF),
        V((LINE, 64, WIDE), F32), V((LINE, 64, WIDE), F32),
        V((8, HALF), F32), V((LINE, 8, HALF), F32),
        V((LINE, 8, WIDE + HALF), F32), V((LINE, 8, WIDE + HALF), F32),
        V((8, WIDE + HALF), F32), V((LINE, 8, WIDE + HALF), F32),
        V((LINE, 8, WIDE), F32),
        V((LINE, 64, WIDE), F32),
        pltpu.SemaphoreType.DMA((N_SEM,)),
        pltpu.SemaphoreType.DMA((N_SEM,)),
    ]
    nodes, weights, bsum = pl.pallas_call(
        kernel,
        out_shape=(
            jax.ShapeDtypeStruct((ROWS, WIDE), F32),
            jax.ShapeDtypeStruct((2 * WIDE, WIDE), F32),
            jax.ShapeDtypeStruct((8, HALF), F32),
        ),
        in_specs=[vmem] * 5 + [smem] + [vmem] * 4,
        out_specs=(vmem, vmem, vmem),
        scratch_shapes=scratch,
        compiler_params=pltpu.CompilerParams(
            collective_id=0, has_side_effects=True, vmem_limit_bytes=48 << 20
        ),
    )(
        agg_feats, out_grad, w_in, w_out, bias_in.reshape(1, WIDE), self_weight, idx_a, idx_b, dst, src
    )
    scale = float(64 * LINE * ROWS) ** -0.5
    weights = weights * scale
    return nodes, weights[:WIDE], weights[WIDE:], bsum[:2].reshape(WIDE) * scale


def solution(mesh):
    placed = (
        P(("dom", "rep"), None), P(("dom", "rep"), None), P(), P(), P(), P(),
        P("dom", "rep", None, None), P("dom", "rep", None), P("dom", "rep", None),
    )
    return jax.shard_map(
        body, mesh=mesh, in_specs=placed, out_specs=(P(("dom", "rep"), None), P(), P(), P()), check_vma=False
    )
```

time: 473 us -> 89.2 us (0.19)
  the two profiles are of different devices: /device:TPU:17 before, /device:TPU:1 now
where the time goes in v1:
time: 89.2 us; the launch traced here: 88.9 us
  Pallas kernels  83.5 us (94%)
  local copies, waits for them, and re-layouts  3.32 us (4%)
  between operations  1.44 us (2%)
    pallas_call x1, Pallas kernels, body(): pl.pallas_call(kernel, out_shape=(jax.ShapeDtypeStruct((ROWS, WIDE), F32)...  83.5 us
    unnamed x17, local copies, waits for them, and re-layouts  2.17 us

profile of v1, /device:TPU:1, one launch (start us, length us, event | category | flops | bytes accessed | tf_op | source)
XLA Modules:
  0.0 88.9 jit_solution(16657548246058842061)
XLA Ops:
  0.7 0.0 copy-start.7
  1.4 0.0 copy-done.7
  1.4 0.0 copy-start.6
  1.4 0.1 copy.15
  1.5 0.6 copy-done.6
  2.1 0.1 copy.16
  2.2 0.0 copy-start.3
  2.2 0.0 copy-start.4
  2.3 0.0 copy-start
  2.3 0.0 copy-start.1
  2.3 0.1 tile.9
  2.4 0.0 copy-start.2
  2.4 0.0 copy-start.5
  2.5 0.6 copy-done.3
  3.0 0.0 copy-done.4
  3.1 0.1 copy-done
  3.2 0.1 copy-done.1
  3.2 0.0 copy-done.2
  3.3 0.0 copy-done.5
  3.3 83.5 %shard_map.120 = (f32[128,256]{1,0:T(8,128)S(1)}, f32[512,256]{1,0:T(8,128)S(1)}, f32[8,128]{1,0:T(8,128)S(1)}) custom-call(bf16[128,256]{1,0:T(8,128)(2,1)S(1)} %copy-done.2, bf16[128,256]{1,0:T(8,128)(2,1)S(1)} %copy-done.3, bf16[256,256]{1,0:T(8,128)(2,1)S(1)} %copy-done, bf16[256,256]{1,0:T(8,128)(2,1)S(1)} %copy-done.1, f32[1,256]{1,0:T(1,128)S(1)} %bitcast.12, ...), custom_call_target="tpu_custom_call" | custom-call | tf_op jit(solution)/shard_map/pallas_call | solution.py:412
  86.8 0.6 multiply_bitcast_fusion
  87.4 0.8 fusion
  88.2 0.7 copy.20
  (6 shorter events, 0.1 us)
Async XLA Ops:
  0.7 0.7 copy-start.7
  1.4 0.7 copy-start.6
  2.2 0.8 copy-start.3
  2.2 0.8 copy-start.4
  2.3 0.9 %copy-start = (bf16[256,256]{1,0:T(8,128)(2,1)S(1)}, bf16[256,256]{1,0:T(8,128)(2,1)}, u32[]{:S(2)}) copy-start(bf16[256,256]{1,0:T(8,128)(2,1)} %w_in_ref.1) | copy-start | bytes 393220
  2.3 1.0 %copy-start.1 = (bf16[256,256]{1,0:T(8,128)(2,1)S(1)}, bf16[256,256]{1,0:T(8,128)(2,1)}, u32[]{:S(2)}) copy-start(bf16[256,256]{1,0:T(8,128)(2,1)} %w_out_ref.1) | copy-start | bytes 393220
  2.4 0.9 copy-start.2
  2.4 0.8 copy-start.5

commit v2 on v1

v2 whole, which is shorter than its diff:
```python
import functools

import jax
import jax.numpy as jnp
from jax import lax
from jax.experimental import pallas as pl
from jax.experimental.pallas import tpu as pltpu
from jax.sharding import PartitionSpec as P

MESH = pl.DeviceIdType.MESH
BF = jnp.bfloat16
F32 = jnp.float32

LINE = 8
ROWS = 128
SLOT = 32
HALF = 128
WIDE = 256
EDGES = 4096
ORDER = (0, 1, 7, 2, 6, 3, 5, 4)
FWD = ((0, 1), (7, 2), (6, 3), (5,), (4,))
BWD = ((1,), (7, 2), (6, 3), (5, 4, 0))

STAGES = (
    "idx_a", "idx_b", "group", "w_rep", "b_rep", "w_z", "w_y", "w_zg", "w_repg",
    "back_a", "back_b", "gsum", "last_a", "last_b",
)
SEM = {name: i for i, name in enumerate(STAGES)}
TWO_A = len(STAGES)
TWO_B = TWO_A + len(FWD)
ONE_A = TWO_B + len(FWD)
ONE_B = ONE_A + LINE
N_SEM = ONE_B + LINE


def each(step):
    for j in ORDER[1:]:
        step(j)


def dot(a, b, dims=((1,), (0,))):
    return lax.dot_general(a, b, (dims, ((), ())), preferred_element_type=F32)


def kernel(
    agg_ref, og_ref, w_in_ref, w_out_ref, bias_ref, sw_ref, idx_a_ref, idx_b_ref, dst_ref, src_ref,
    nodes_ref, weights_ref, bsum_ref,
    ga_ref, grp, blk_a, blk_b, ia, ib, pt_a, pt_b, pc_a, pc_b, stage_a, stage_b, mir_a, mir_b,
    v_dst, v_src, fetched, out_a, out_b, ra, rb, last_src_a, last_src_b, fa, fb, gout, gin,
    wsend, wrecv, bsend, brecv, zsend, zrecv, ysend, yrecv, zg, wfull, ssem, rsem,
):
    me = lax.axis_index("dom")
    r = lax.axis_index("rep")
    z, y = me // LINE, me % LINE
    z_at, y_at, r_at = ([lax.rem(own + j, LINE) for j in range(LINE)] for own in (z, y, r))

    def on_z(to):
        return (to * LINE + y, r)

    def on_y(to):
        return (z * LINE + to, r)

    def on_rep(to):
        return (me, to)

    def send(src, dst, sem, device):
        pltpu.make_async_remote_copy(
            src_ref=src, dst_ref=dst, send_sem=ssem.at[sem], recv_sem=rsem.at[sem],
            device_id=device, device_id_type=MESH,
        ).start()

    def got(view, sem):
        pltpu.make_async_copy(view, view, rsem.at[sem]).wait()

    def sent(view, sem):
        pltpu.make_async_copy(view, view, ssem.at[sem]).wait()

    barrier = pltpu.get_barrier_semaphore()

    def greet(j):
        for device in (on_z(z_at[j]), on_y(y_at[j]), on_rep(r_at[j])):
            pl.semaphore_signal(barrier, inc=1, device_id=device, device_id_type=MESH)

    each(greet)

    agg, og = agg_ref[...], og_ref[...]
    preact = dot(agg, w_in_ref[...]) + bias_ref[...]
    gated = jax.nn.sigmoid(preact)
    back_act = dot(og, w_out_ref[...], ((1,), (1,)))
    grad_pre = (back_act * gated * (1.0 + preact * (1.0 - gated))).astype(BF)
    grad_agg = dot(grad_pre, w_in_ref[...], ((1,), (1,))).astype(BF)
    ga_ref[...] = grad_agg
    grp[r] = grad_agg
    blk_a[z] = grad_agg[:, :HALF]
    blk_b[y] = grad_agg[:, HALF:]
    ia[y] = idx_a_ref[y]
    ib[z] = idx_b_ref[z]

    pl.semaphore_wait(barrier, 3 * (LINE - 1))

    def send_idx(j):
        to = y_at[j]
        send(idx_a_ref.at[to], ia.at[y], SEM["idx_a"], on_y(to))
        to = z_at[j]
        send(idx_b_ref.at[to], ib.at[z], SEM["idx_b"], on_z(to))

    each(send_idx)

    def send_blocks(j):
        send(blk_a.at[z], blk_a.at[z], ONE_A + LINE - j, on_z(z_at[j]))
        send(blk_b.at[y], blk_b.at[y], ONE_B + LINE - j, on_y(y_at[j]))

    each(send_blocks)

    activated = (preact * gated).astype(BF)
    g_in = dot(agg, grad_pre, ((0,), (0,)))
    g_out = dot(activated, og, ((0,), (0,)))
    wsend[0:4] = g_in.astype(BF).reshape(4, 64, WIDE)
    wsend[4:8] = g_out.astype(BF).reshape(4, 64, WIDE)
    column_sums = jnp.sum(grad_pre.astype(F32), axis=0, keepdims=True)
    row = lax.broadcasted_iota(jnp.int32, (8, HALF), 0)
    bsend[...] = jnp.where(
        row == 0, column_sums[:, :HALF], jnp.where(row == 1, column_sums[:, HALF:], 0.0)
    )

    def send_weights(j):
        to = r_at[j]
        send(wsend.at[to], wrecv.at[r], SEM["w_rep"], on_rep(to))
        send(bsend, brecv.at[r], SEM["b_rep"], on_rep(to))

    each(send_weights)

    def send_group(j):
        send(grp.at[r], grp.at[r], SEM["group"], on_rep(r_at[j]))

    each(send_group)
    wrecv[r] = wsend[r]
    brecv[r] = bsend[...]

    got(ia.at[0:7], SEM["idx_a"])
    got(ib.at[0:7], SEM["idx_b"])
    sub = lax.broadcasted_iota(jnp.int32, (ROWS, WIDE), 0)
    lane = lax.broadcasted_iota(jnp.int32, (WIDE, ROWS), 1)
    for came, picks, columns in ((ia, pt_a, pc_a), (ib, pt_b, pc_b)):
        parts = []
        for g in range(2):
            part = came[4 * g]
            for i in range(1, 4):
                part = jnp.maximum(part, came[4 * g + i])
            parts.append(part)
        both = jnp.concatenate(parts, axis=1)
        for i in range(LINE):
            picks[i] = jnp.where(sub == both[i : i + 1, :], 1.0, 0.0).astype(BF)
        both = both.T
        for i in range(LINE):
            columns[i] = jnp.where(lane == both[:, i : i + 1], 1.0, 0.0).astype(BF)

    chunk_of = {j: c for c, offsets in enumerate(FWD) for j in offsets}
    for j in ORDER:
        block = z_at[j]
        if j:
            got(blk_a.at[0], ONE_A + j)
        rows = dot(pc_a[block], blk_a[block]).astype(BF)
        stage_a[:, block] = rows.reshape(LINE, SLOT, HALF)

        def send_a(j, block=block, c=chunk_of[j]):
            to = y_at[j]
            send(stage_a.at[to, block], mir_a.at[block, y], TWO_A + c, on_y(to))

        each(send_a)
        block = y_at[j]
        if j:
            got(blk_b.at[0], ONE_B + j)
        rows = dot(pc_b[block], blk_b[block]).astype(BF)
        stage_b[:, block] = rows.reshape(LINE, SLOT, HALF)
    got(wrecv.at[0:7], SEM["w_rep"])
    got(brecv.at[0:7], SEM["b_rep"])
    total = wrecv[0].astype(F32)
    bias_total = brecv[0]
    for i in range(1, LINE):
        total = total + wrecv[i].astype(F32)
        bias_total = bias_total + brecv[i]
    zsend[:, :, :WIDE] = total.reshape(LINE, 8, WIDE)
    zsend[:, :, WIDE:] = jnp.broadcast_to(bias_total[None], (LINE, 8, HALF))

    def send_z(j):
        to = z_at[j]
        send(zsend.at[to], zrecv.at[z], SEM["w_z"], on_z(to))

    each(send_z)
    zrecv[z] = zsend[z]

    for j in ORDER[1:]:
        to = z_at[LINE - j]
        send(stage_b.at[to], mir_b.at[z], TWO_B + chunk_of[j], on_z(to))
    mir_b[z] = stage_b[z]
    mir_a[:, y] = stage_a[y]

    lane = lax.broadcasted_iota(jnp.int32, (ROWS, ROWS), 1)
    for c in range(EDGES // ROWS):
        col = dst_ref[:, c : c + 1]
        v_dst[c * ROWS : (c + 1) * ROWS, :] = jnp.where((col & 127) == lane, col >> 7, -1).astype(BF)
    sub = lax.broadcasted_iota(jnp.int32, (ROWS, 512), 0)
    for c in range(EDGES // 512):
        cut = src_ref[:, c * 512 : (c + 1) * 512]
        v_src[:, c * 512 : (c + 1) * 512] = jnp.where((cut & 127) == sub, cut >> 7, -1).astype(BF)

    def one_hot(codes, high):
        if not isinstance(high, int):
            high = high.astype(F32)
        return jnp.where(codes == jnp.asarray(high, F32).astype(BF), BF(1), BF(0))

    got(grp.at[0:7], SEM["group"])
    hot = jnp.concatenate([one_hot(v_dst[...], h) for h in range(LINE)], axis=1)
    fetched[...] = dot(hot, grp[...].reshape(LINE * ROWS, WIDE)).astype(BF)

    got(zrecv.at[0:7], SEM["w_z"])
    total = zrecv[0]
    for i in range(1, LINE):
        total = total + zrecv[i]
    ysend[...] = total

    def send_y(j):
        send(ysend, yrecv.at[y], SEM["w_y"], on_y(y_at[j]))

    each(send_y)
    yrecv[y] = total

    def gather_mirrors(c):
        offsets = FWD[c]
        got(mir_b.at[0 : len([j for j in offsets if j])], TWO_B + c)
        got(mir_a.at[0 : len(offsets), 0:7], TWO_A + c)
        blocks = [z_at[j] for j in offsets]
        values = jnp.concatenate(
            [
                jnp.concatenate([mir_a[block].reshape(WIDE, HALF), mir_b[block].reshape(WIDE, HALF)], axis=1)
                for block in blocks
            ],
            axis=0,
        )
        hot = jnp.concatenate(
            [one_hot(v_dst[...], 8 + 2 * block + h) for block in blocks for h in range(2)], axis=1
        )
        fetched[...] = fetched[...] + dot(hot, values).astype(BF)

    for c in range(len(FWD)):
        gather_mirrors(c)

    got(yrecv.at[0:7], SEM["w_y"])
    total = yrecv[0]
    for i in range(1, LINE):
        total = total + yrecv[i]
    bsum_ref[...] = total[:, WIDE:]
    zg[z] = total[:, :WIDE]

    def send_zg(j):
        send(zg.at[z], zg.at[z], SEM["w_zg"], on_z(z_at[j]))

    each(send_zg)

    for c, offsets in enumerate(BWD):
        blocks = [z_at[j] for j in offsets]
        hot = jnp.concatenate(
            [one_hot(v_src[...], 8 + 2 * block + h) for block in blocks for h in range(2)], axis=0
        )
        sums = dot(hot, fetched[...]).astype(BF)
        for n, (j, block) in enumerate(zip(offsets, blocks)):
            part = sums[n * WIDE : (n + 1) * WIDE]
            out_a[block] = part[:, :HALF].reshape(LINE, SLOT, HALF)
            out_b[block] = part[:, HALF:].reshape(LINE, SLOT, HALF)
            if j:
                send(out_b.at[block], rb.at[z], SEM["back_b"], on_z(block))
            else:
                rb[z] = out_b[block]
            ra[y, block] = out_a[block, y]

            def send_back(j, block=block):
                to = y_at[j]
                send(out_a.at[block, to], ra.at[y, block], SEM["back_a"], on_y(to))

            each(send_back)
        if c != 1:
            continue

        got(zg.at[0:7], SEM["w_zg"])
        wfull[r] = zg[...].reshape(64, WIDE)

        def send_full(j):
            send(wfull.at[r], wfull.at[r], SEM["w_repg"], on_rep(r_at[j]))

        each(send_full)

    for c in range(2):
        hot = jnp.concatenate([one_hot(v_src[...], 4 * c + h) for h in range(4)], axis=0)
        gout[4 * c : 4 * c + 4] = dot(hot, fetched[...]).astype(BF).reshape(4, ROWS, WIDE)

    def send_sums(j):
        to = r_at[j]
        send(gout.at[to], gin.at[r], SEM["gsum"], on_rep(to))

    each(send_sums)
    gin[r] = gout[r]

    got(rb.at[0:7], SEM["back_b"])

    for i in range(LINE):
        sums = dot(pt_b[i], rb[:, i].reshape(WIDE, HALF))
        last_src_b[i] = sums.astype(BF)
    fb[y] = last_src_b[y]

    def send_last_b(j):
        to = y_at[j]
        send(last_src_b.at[to], fb.at[y], SEM["last_b"], on_y(to))

    each(send_last_b)
    got(ra.at[0:7], SEM["back_a"])

    for i in range(LINE):
        sums = dot(pt_a[i], ra[:, i].reshape(WIDE, HALF))
        last_src_a[i] = sums.astype(BF)
    fa[z] = last_src_a[z]

    def send_last_a(j):
        to = z_at[j]
        send(last_src_a.at[to], fa.at[z], SEM["last_a"], on_z(to))

    each(send_last_a)

    nodes = (1.0 + sw_ref[0]) * ga_ref[...].astype(F32)
    got(gin.at[0:7], SEM["gsum"])
    for i in range(LINE):
        nodes = nodes + gin[i].astype(F32)
    got(wfull.at[0:7], SEM["w_repg"])
    weights_ref[...] = wfull[...].reshape(LINE * 64, WIDE)
    got(fb.at[0:7], SEM["last_b"])
    right = nodes[:, HALF:]
    for i in range(LINE):
        right = right + fb[i].astype(F32)
    nodes_ref[:, HALF:] = right
    got(fa.at[0:7], SEM["last_a"])
    left = nodes[:, :HALF]
    for i in range(LINE):
        left = left + fa[i].astype(F32)
    nodes_ref[:, :HALF] = left

    for view, name in (
        (ia, "idx_a"), (ib, "idx_b"), (grp, "group"), (wrecv, "w_rep"),
        (brecv, "b_rep"), (zrecv, "w_z"), (yrecv, "w_y"), (zg, "w_zg"), (wfull, "w_repg"), (ra, "back_a"),
        (rb, "back_b"), (gin, "gsum"), (fa, "last_a"), (fb, "last_b"),
    ):
        sent(view.at[0:7], SEM[name])
    for j in range(1, LINE):
        sent(blk_a.at[0], ONE_A + j)
        sent(blk_b.at[0], ONE_B + j)
    for c, offsets in enumerate(FWD):
        sent(mir_b.at[0 : len([j for j in offsets if j])], TWO_B + c)
        sent(mir_a.at[0 : len(offsets), 0:7], TWO_A + c)


def body(agg_feats, out_grad, w_in, w_out, bias_in, self_weight, mirror_rows, edge_src, edge_dst):
    me = lax.axis_index("dom")
    r = lax.axis_index("rep")
    z, y = me // LINE, me % LINE
    rows = mirror_rows[0, 0] - r * ROWS
    rows = jnp.tile(rows, (1, 4)).reshape(LINE, LINE, ROWS)
    quarter = lax.broadcasted_iota(jnp.int32, (1, 1, ROWS), 2) // SLOT
    idx_a = jnp.where(quarter == y % 4, rows.swapaxes(0, 1), -1)
    idx_b = jnp.where(quarter == z % 4, rows, -1)
    dst = edge_dst.reshape(EDGES // ROWS, ROWS).T
    src = edge_src.reshape(1, EDGES)

    vmem = pl.BlockSpec(memory_space=pltpu.VMEM)
    smem = pl.BlockSpec(memory_space=pltpu.SMEM)
    V = pltpu.VMEM
    scratch = [
        V((ROWS, WIDE), BF),
        V((LINE, ROWS, WIDE), BF),
        V((LINE, ROWS, HALF), BF), V((LINE, ROWS, HALF), BF),
        V((LINE, LINE, ROWS), jnp.int32), V((LINE, LINE, ROWS), jnp.int32),
        V((LINE, ROWS, WIDE), BF), V((LINE, ROWS, WIDE), BF),
        V((LINE, WIDE, ROWS), BF), V((LINE, WIDE, ROWS), BF),
        V((LINE, LINE, SLOT, HALF), BF), V((LINE, LINE, SLOT, HALF), BF),
        V((LINE, LINE, SLOT, HALF), BF), V((LINE, LINE, SLOT, HALF), BF),
        V((EDGES, ROWS), BF), V((ROWS, EDGES), BF),
        V((EDGES, WIDE), BF),
        V((LINE, LINE, SLOT, HALF), BF), V((LINE, LINE, SLOT, HALF), BF),
        V((LINE, LINE, SLOT, HALF), BF), V((LINE, LINE, SLOT, HALF), BF),
        V((LINE, ROWS, HALF), BF), V((LINE, ROWS, HALF), BF),
        V((LINE, ROWS, HALF), BF), V((LINE, ROWS, HALF), BF),
        V((LINE, ROWS, WIDE), BF), V((LINE, ROWS, WIDE), BF),
        V((LINE, 64, WIDE), BF), V((LINE, 64, WIDE), BF),
        V((8, HALF), F32), V((LINE, 8, HALF), F32),
        V((LINE, 8, WIDE + HALF), F32), V((LINE, 8, WIDE + HALF), F32),
        V((8, WIDE + HALF), F32), V((LINE, 8, WIDE + HALF), F32),
        V((LINE, 8, WIDE), F32),
        V((LINE, 64, WIDE), F32),
        pltpu.SemaphoreType.DMA((N_SEM,)),
        pltpu.SemaphoreType.DMA((N_SEM,)),
    ]
    nodes, weights, bsum = pl.pallas_call(
        kernel,
        out_shape=(
            jax.ShapeDtypeStruct((ROWS, WIDE), F32),
            jax.ShapeDtypeStruct((2 * WIDE, WIDE), F32),
            jax.ShapeDtypeStruct((8, HALF), F32),
        ),
        in_specs=[vmem] * 5 + [smem] + [vmem] * 4,
        out_specs=(vmem, vmem, vmem),
        scratch_shapes=scratch,
        compiler_params=pltpu.CompilerParams(
            collective_id=0, has_side_effects=True, vmem_limit_bytes=48 << 20
        ),
    )(
        agg_feats, out_grad, w_in, w_out, bias_in.reshape(1, WIDE), self_weight, idx_a, idx_b, dst, src
    )
    scale = float(64 * LINE * ROWS) ** -0.5
    weights = weights * scale
    return nodes, weights[:WIDE], weights[WIDE:], bsum[:2].reshape(WIDE) * scale


def solution(mesh):
    placed = (
        P(("dom", "rep"), None), P(("dom", "rep"), None), P(), P(), P(), P(),
        P("dom", "rep", None, None), P("dom", "rep", None), P("dom", "rep", None),
    )
    return jax.shard_map(
        body, mesh=mesh, in_specs=placed, out_specs=(P(("dom", "rep"), None), P(), P(), P()), check_vma=False
    )
```

time: 89.2 us -> 78.4 us (0.88)
  the two profiles are of different devices: /device:TPU:1 before, /device:TPU:8 now
where the time goes in v2:
time: 78.4 us; the launch traced here: 78.1 us
  Pallas kernels  72.8 us (93%)
  local copies, waits for them, and re-layouts  3.32 us (4%)
  between operations  1.44 us (2%)
    pallas_call x1, Pallas kernels, body(): pl.pallas_call(kernel, out_shape=(jax.ShapeDtypeStruct((ROWS, WIDE), F32)...  72.8 us
    unnamed x17, local copies, waits for them, and re-layouts  2.17 us

profile of v2, /device:TPU:8, one launch (start us, length us, event | category | flops | bytes accessed | tf_op | source)
XLA Modules:
  0.0 78.1 jit_solution(6093128600665640277)
XLA Ops:
  0.7 0.0 copy-start.7
  1.4 0.0 copy-done.7
  1.4 0.0 copy-start.6
  1.4 0.1 copy.15
  1.5 0.6 copy-done.6
  2.1 0.1 copy.16
  2.2 0.0 copy-start.3
  2.2 0.0 copy-start.4
  2.3 0.0 copy-start
  2.3 0.0 copy-start.1
  2.3 0.1 tile.9
  2.4 0.0 copy-start.2
  2.4 0.0 copy-start.5
  2.5 0.6 copy-done.3
  3.0 0.0 copy-done.4
  3.1 0.1 copy-done
  3.2 0.1 copy-done.1
  3.2 0.0 copy-done.2
  3.3 0.0 copy-done.5
  3.3 72.8 %shard_map.120 = (f32[128,256]{1,0:T(8,128)S(1)}, f32[512,256]{1,0:T(8,128)S(1)}, f32[8,128]{1,0:T(8,128)S(1)}) custom-call(bf16[128,256]{1,0:T(8,128)(2,1)S(1)} %copy-done.2, bf16[128,256]{1,0:T(8,128)(2,1)S(1)} %copy-done.3, bf16[256,256]{1,0:T(8,128)(2,1)S(1)} %copy-done, bf16[256,256]{1,0:T(8,128)(2,1)S(1)} %copy-done.1, f32[1,256]{1,0:T(1,128)S(1)} %bitcast.12, ...), custom_call_target="tpu_custom_call" | custom-call | tf_op jit(solution)/shard_map/pallas_call | solution.py:400
  76.0 0.6 multiply_bitcast_fusion
  76.6 0.8 %fusion = (f32[256,256]{1,0:T(8,128)}, f32[256,256]{1,0:T(8,128)}) fusion(f32[512,256]{1,0:T(8,128)S(1)} %broadcast_multiply_fusion), kind=kLoop, calls=%fused_computation.11 | loop fusion | bytes 1048576 | tf_op jit(solution)/shard_map/slice | solution.py:418
  77.5 0.7 copy.20
  (6 shorter events, 0.1 us)
Async XLA Ops:
  0.7 0.7 copy-start.7
  1.4 0.7 copy-start.6
  2.2 0.8 %copy-start.3 = (bf16[128,256]{1,0:T(8,128)(2,1)S(1)}, bf16[128,256]{1,0:T(8,128)(2,1)}, u32[]{:S(2)}) copy-start(bf16[128,256]{1,0:T(8,128)(2,1)} %og_ref.1) | copy-start | bytes 196612
  2.2 0.8 %copy-start.4 = (s32[1,1,4096]{2,1,0:T(1,128)S(1)}, s32[1,1,4096]{2,1,0:T(1,128)}, u32[]{:S(2)}) copy-start(s32[1,1,4096]{2,1,0:T(1,128)} %param.16) | copy-start | bytes 49156
  2.3 0.9 %copy-start = (bf16[256,256]{1,0:T(8,128)(2,1)S(1)}, bf16[256,256]{1,0:T(8,128)(2,1)}, u32[]{:S(2)}) copy-start(bf16[256,256]{1,0:T(8,128)(2,1)} %w_in_ref.1) | copy-start | bytes 393220
  2.3 1.0 %copy-start.1 = (bf16[256,256]{1,0:T(8,128)(2,1)S(1)}, bf16[256,256]{1,0:T(8,128)(2,1)}, u32[]{:S(2)}) copy-start(bf16[256,256]{1,0:T(8,128)(2,1)} %w_out_ref.1) | copy-start | bytes 393220
  2.4 0.9 %copy-start.2 = (bf16[128,256]{1,0:T(8,128)(2,1)S(1)}, bf16[128,256]{1,0:T(8,128)(2,1)}, u32[]{:S(2)}) copy-start(bf16[128,256]{1,0:T(8,128)(2,1)} %agg_ref.1) | copy-start | bytes 196612
  2.4 0.8 %copy-start.5 = (f32[256]{0:T(256)S(1)}, f32[256]{0:T(256)}, u32[]{:S(2)}) copy-start(f32[256]{0:T(256)} %param.13) | copy-start | bytes 3076

commit v3 on v2

--- a/solution.py
+++ b/solution.py
@@ -173,22 +173,25 @@
             got(blk_b.at[0], ONE_B + j)
         rows = dot(pc_b[block], blk_b[block]).astype(BF)
         stage_b[:, block] = rows.reshape(LINE, SLOT, HALF)
-    got(wrecv.at[0:7], SEM["w_rep"])
-    got(brecv.at[0:7], SEM["b_rep"])
-    total = wrecv[0].astype(F32)
-    bias_total = brecv[0]
-    for i in range(1, LINE):
-        total = total + wrecv[i].astype(F32)
-        bias_total = bias_total + brecv[i]
-    zsend[:, :, :WIDE] = total.reshape(LINE, 8, WIDE)
-    zsend[:, :, WIDE:] = jnp.broadcast_to(bias_total[None], (LINE, 8, HALF))
-
-    def send_z(j):
-        to = z_at[j]
-        send(zsend.at[to], zrecv.at[z], SEM["w_z"], on_z(to))
-
-    each(send_z)
-    zrecv[z] = zsend[z]
+        if j != 5:
+            continue
+
+        got(wrecv.at[0:7], SEM["w_rep"])
+        got(brecv.at[0:7], SEM["b_rep"])
+        total = wrecv[0].astype(F32)
+        bias_total = brecv[0]
+        for i in range(1, LINE):
+            total = total + wrecv[i].astype(F32)
+            bias_total = bias_total + brecv[i]
+        zsend[:, :, :WIDE] = total.reshape(LINE, 8, WIDE)
+        zsend[:, :, WIDE:] = jnp.broadcast_to(bias_total[None], (LINE, 8, HALF))
+
+        def send_z(j):
+            to = z_at[j]
+            send(zsend.at[to], zrecv.at[z], SEM["w_z"], on_z(to))
+
+        each(send_z)
+        zrecv[z] = zsend[z]
 
     for j in ORDER[1:]:
         to = z_at[LINE - j]
@@ -197,8 +200,9 @@
     mir_a[:, y] = stage_a[y]
 
     lane = lax.broadcasted_iota(jnp.int32, (ROWS, ROWS), 1)
+    targets = dst_ref[...].T
     for c in range(EDGES // ROWS):
-        col = dst_ref[:, c : c + 1]
+        col = targets[:, c : c + 1]
         v_dst[c * ROWS : (c + 1) * ROWS, :] = jnp.where((col & 127) == lane, col >> 7, -1).astype(BF)
     sub = lax.broadcasted_iota(jnp.int32, (ROWS, 512), 0)
     for c in range(EDGES // 512):
@@ -213,18 +217,6 @@
     got(grp.at[0:7], SEM["group"])
     hot = jnp.concatenate([one_hot(v_dst[...], h) for h in range(LINE)], axis=1)
     fetched[...] = dot(hot, grp[...].reshape(LINE * ROWS, WIDE)).astype(BF)
-
-    got(zrecv.at[0:7], SEM["w_z"])
-    total = zrecv[0]
-    for i in range(1, LINE):
-        total = total + zrecv[i]
-    ysend[...] = total
-
-    def send_y(j):
-        send(ysend, yrecv.at[y], SEM["w_y"], on_y(y_at[j]))
-
-    each(send_y)
-    yrecv[y] = total
 
     def gather_mirrors(c):
         offsets = FWD[c]
@@ -243,7 +235,21 @@
         )
         fetched[...] = fetched[...] + dot(hot, values).astype(BF)
 
-    for c in range(len(FWD)):
+    gather_mirrors(0)
+
+    got(zrecv.at[0:7], SEM["w_z"])
+    total = zrecv[0]
+    for i in range(1, LINE):
+        total = total + zrecv[i]
+    ysend[...] = total
+
+    def send_y(j):
+        send(ysend, yrecv.at[y], SEM["w_y"], on_y(y_at[j]))
+
+    each(send_y)
+    yrecv[y] = total
+
+    for c in range(1, len(FWD)):
         gather_mirrors(c)
 
     got(yrecv.at[0:7], SEM["w_y"])
@@ -279,7 +285,7 @@
                 send(out_a.at[block, to], ra.at[y, block], SEM["back_a"], on_y(to))
 
             each(send_back)
-        if c != 1:
+        if c != 3:
             continue
 
         got(zg.at[0:7], SEM["w_zg"])
@@ -366,7 +372,7 @@
     quarter = lax.broadcasted_iota(jnp.int32, (1, 1, ROWS), 2) // SLOT
     idx_a = jnp.where(quarter == y % 4, rows.swapaxes(0, 1), -1)
     idx_b = jnp.where(quarter == z % 4, rows, -1)
-    dst = edge_dst.reshape(EDGES // ROWS, ROWS).T
+    dst = edge_dst.reshape(EDGES // ROWS, ROWS)
     src = edge_src.reshape(1, EDGES)
 
     vmem = pl.BlockSpec(memory_space=pltpu.VMEM)

time: 78.4 us -> 72.8 us (0.929)
  the two profiles are of different devices: /device:TPU:8 before, /device:TPU:2 now
where the time goes in v3:
time: 72.8 us; the launch traced here: 72.6 us
  Pallas kernels  68 us (93%)
  local copies, waits for them, and re-layouts  2.59 us (4%)
  between operations  1.44 us (2%)
    pallas_call x1, Pallas kernels, body(): pl.pallas_call(kernel, out_shape=(jax.ShapeDtypeStruct((ROWS, WIDE), F32)...  68 us
    unnamed x17, local copies, waits for them, and re-layouts  1.54 us

profile of v3, /device:TPU:2, one launch (start us, length us, event | category | flops | bytes accessed | tf_op | source)
XLA Modules:
  0.0 72.6 jit_solution(4897799536330889921)
XLA Ops:
  0.7 0.0 copy-start.7
  1.4 0.0 copy-done.7
  1.4 0.1 copy.15
  1.5 0.0 copy-start.3
  1.5 0.0 copy-start.4
  1.5 0.0 copy-start.5
  1.5 0.0 copy-start
  1.5 0.0 copy-start.1
  1.6 0.1 tile.9
  1.7 0.0 copy-start.2
  1.7 0.0 copy-start.6
  1.7 0.6 copy-done.3
  2.3 0.0 copy-done.4
  2.3 0.0 copy-done.5
  2.3 0.1 copy-done
  2.5 0.1 copy-done.1
  2.5 0.0 copy-done.2
  2.6 0.0 copy-done.6
  2.6 68.0 %shard_map.120 = (f32[128,256]{1,0:T(8,128)S(1)}, f32[512,256]{1,0:T(8,128)S(1)}, f32[8,128]{1,0:T(8,128)S(1)}) custom-call(bf16[128,256]{1,0:T(8,128)(2,1)S(1)} %copy-done.2, bf16[128,256]{1,0:T(8,128)(2,1)S(1)} %copy-done.3, bf16[256,256]{1,0:T(8,128)(2,1)S(1)} %copy-done, bf16[256,256]{1,0:T(8,128)(2,1)S(1)} %copy-done.1, f32[1,256]{1,0:T(1,128)S(1)} %bitcast.11, ...), custom_call_target="tpu_custom_call" | custom-call | tf_op jit(solution)/shard_map/pallas_call | solution.py:406
  70.6 0.6 multiply_bitcast_fusion
  71.2 0.8 %fusion = (f32[256,256]{1,0:T(8,128)}, f32[256,256]{1,0:T(8,128)}) fusion(f32[512,256]{1,0:T(8,128)S(1)} %broadcast_multiply_fusion), kind=kLoop, calls=%fused_computation.11 | loop fusion | bytes 1048576 | tf_op jit(solution)/shard_map/slice | solution.py:424
  72.0 0.7 copy.19
  (6 shorter events, 0.1 us)
Async XLA Ops:
  0.7 0.7 copy-start.7
  1.5 0.8 %copy-start.3 = (bf16[128,256]{1,0:T(8,128)(2,1)S(1)}, bf16[128,256]{1,0:T(8,128)(2,1)}, u32[]{:S(2)}) copy-start(bf16[128,256]{1,0:T(8,128)(2,1)} %og_ref.1) | copy-start | bytes 196612
  1.5 0.8 %copy-start.4 = (s32[1,1,4096]{2,1,0:T(1,128)S(1)}, s32[1,1,4096]{2,1,0:T(1,128)}, u32[]{:S(2)}) copy-start(s32[1,1,4096]{2,1,0:T(1,128)} %param.17) | copy-start | bytes 49156
  1.5 0.8 %copy-start.5 = (s32[1,1,4096]{2,1,0:T(1,128)S(1)}, s32[1,1,4096]{2,1,0:T(1,128)}, u32[]{:S(2)}) copy-start(s32[1,1,4096]{2,1,0:T(1,128)} %param.16) | copy-start | bytes 49156
  1.5 0.9 %copy-start = (bf16[256,256]{1,0:T(8,128)(2,1)S(1)}, bf16[256,256]{1,0:T(8,128)(2,1)}, u32[]{:S(2)}) copy-start(bf16[256,256]{1,0:T(8,128)(2,1)} %w_in_ref.1) | copy-start | bytes 393220
  1.5 1.0 %copy-start.1 = (bf16[256,256]{1,0:T(8,128)(2,1)S(1)}, bf16[256,256]{1,0:T(8,128)(2,1)}, u32[]{:S(2)}) copy-start(bf16[256,256]{1,0:T(8,128)(2,1)} %w_out_ref.1) | copy-start | bytes 393220
  1.7 0.9 %copy-start.2 = (bf16[128,256]{1,0:T(8,128)(2,1)S(1)}, bf16[128,256]{1,0:T(8,128)(2,1)}, u32[]{:S(2)}) copy-start(bf16[128,256]{1,0:T(8,128)(2,1)} %agg_ref.1) | copy-start | bytes 196612
  1.7 0.8 %copy-start.6 = (f32[256]{0:T(256)S(1)}, f32[256]{0:T(256)}, u32[]{:S(2)}) copy-start(f32[256]{0:T(256)} %param.13) | copy-start | bytes 3076

commit v4 on v3

--- a/solution.py
+++ b/solution.py
@@ -19,7 +19,7 @@
 EDGES = 4096
 ORDER = (0, 1, 7, 2, 6, 3, 5, 4)
 FWD = ((0, 1), (7, 2), (6, 3), (5,), (4,))
-BWD = ((1,), (7, 2), (6, 3), (5, 4, 0))
+BWD = ((1, 7), (2, 6), (3, 5), (4, 0))
 
 STAGES = (
     "idx_a", "idx_b", "group", "w_rep", "b_rep", "w_z", "w_y", "w_zg", "w_repg",

time: 72.8 us -> 72.5 us (level)
  no operation moved by 1% of the time
where the time goes in v4:
time: 72.5 us; the launch traced here: 72.3 us
  Pallas kernels  67.6 us (93%)
  local copies, waits for them, and re-layouts  2.59 us (4%)
  between operations  1.44 us (2%)
    pallas_call x1, Pallas kernels, body(): pl.pallas_call(kernel, out_shape=(jax.ShapeDtypeStruct((ROWS, WIDE), F32)...  67.6 us
    unnamed x17, local copies, waits for them, and re-layouts  1.54 us

profile of v4, /device:TPU:2, one launch (start us, length us, event | category | flops | bytes accessed | tf_op | source)
XLA Modules:
  0.0 72.3 jit_solution(15709076272084155603)
XLA Ops:
  0.7 0.0 copy-start.7
  1.4 0.0 copy-done.7
  1.4 0.1 copy.15
  1.5 0.0 copy-start.3
  1.5 0.0 copy-start.4
  1.5 0.0 copy-start.5
  1.5 0.0 copy-start
  1.5 0.0 copy-start.1
  1.6 0.1 tile.9
  1.7 0.0 copy-start.2
  1.7 0.0 copy-start.6
  1.7 0.6 copy-done.3
  2.3 0.0 copy-done.4
  2.3 0.0 copy-done.5
  2.3 0.1 copy-done
  2.5 0.1 copy-done.1
  2.5 0.0 copy-done.2
  2.6 0.0 copy-done.6
  2.6 67.6 %shard_map.120 = (f32[128,256]{1,0:T(8,128)S(1)}, f32[512,256]{1,0:T(8,128)S(1)}, f32[8,128]{1,0:T(8,128)S(1)}) custom-call(bf16[128,256]{1,0:T(8,128)(2,1)S(1)} %copy-done.2, bf16[128,256]{1,0:T(8,128)(2,1)S(1)} %copy-done.3, bf16[256,256]{1,0:T(8,128)(2,1)S(1)} %copy-done, bf16[256,256]{1,0:T(8,128)(2,1)S(1)} %copy-done.1, f32[1,256]{1,0:T(1,128)S(1)} %bitcast.11, ...), custom_call_target="tpu_custom_call" | custom-call | tf_op jit(solution)/shard_map/pallas_call | solution.py:406
  70.2 0.6 multiply_bitcast_fusion
  70.8 0.8 %fusion = (f32[256,256]{1,0:T(8,128)}, f32[256,256]{1,0:T(8,128)}) fusion(f32[512,256]{1,0:T(8,128)S(1)} %broadcast_multiply_fusion), kind=kLoop, calls=%fused_computation.11 | loop fusion | bytes 1048576 | tf_op jit(solution)/shard_map/slice | solution.py:424
  71.6 0.7 copy.19
  (6 shorter events, 0.1 us)
Async XLA Ops:
  0.7 0.7 copy-start.7
  1.5 0.8 %copy-start.3 = (bf16[128,256]{1,0:T(8,128)(2,1)S(1)}, bf16[128,256]{1,0:T(8,128)(2,1)}, u32[]{:S(2)}) copy-start(bf16[128,256]{1,0:T(8,128)(2,1)} %og_ref.1) | copy-start | bytes 196612
  1.5 0.8 %copy-start.4 = (s32[1,1,4096]{2,1,0:T(1,128)S(1)}, s32[1,1,4096]{2,1,0:T(1,128)}, u32[]{:S(2)}) copy-start(s32[1,1,4096]{2,1,0:T(1,128)} %param.17) | copy-start | bytes 49156
  1.5 0.8 %copy-start.5 = (s32[1,1,4096]{2,1,0:T(1,128)S(1)}, s32[1,1,4096]{2,1,0:T(1,128)}, u32[]{:S(2)}) copy-start(s32[1,1,4096]{2,1,0:T(1,128)} %param.16) | copy-start | bytes 49156
  1.5 0.9 %copy-start = (bf16[256,256]{1,0:T(8,128)(2,1)S(1)}, bf16[256,256]{1,0:T(8,128)(2,1)}, u32[]{:S(2)}) copy-start(bf16[256,256]{1,0:T(8,128)(2,1)} %w_in_ref.1) | copy-start | bytes 393220
  1.5 1.0 %copy-start.1 = (bf16[256,256]{1,0:T(8,128)(2,1)S(1)}, bf16[256,256]{1,0:T(8,128)(2,1)}, u32[]{:S(2)}) copy-start(bf16[256,256]{1,0:T(8,128)(2,1)} %w_out_ref.1) | copy-start | bytes 393220
  1.7 0.9 %copy-start.2 = (bf16[128,256]{1,0:T(8,128)(2,1)S(1)}, bf16[128,256]{1,0:T(8,128)(2,1)}, u32[]{:S(2)}) copy-start(bf16[128,256]{1,0:T(8,128)(2,1)} %agg_ref.1) | copy-start | bytes 196612
  1.7 0.8 %copy-start.6 = (f32[256]{0:T(256)S(1)}, f32[256]{0:T(256)}, u32[]{:S(2)}) copy-start(f32[256]{0:T(256)} %param.13) | copy-start | bytes 3076
